TPU v7x, 32 devices: a whole 2x2x4 slice. The times are simulated.
32 devices in a mesh: dom: 16 (over z, x, core), feat: 2 (over y).
Axes of the slice: x: 2, y: 2, z: 4, core: 2. Of those that a mesh axis runs over, the one named last changes fastest.
Arguments:
- fine_latent: bfloat16 [256, 262144], P('feat', 'dom'), may hold values from -6 to 6
- coarse_latent: bfloat16 [256, 131072], P('feat', 'dom'), may hold values from -6 to 6
- parents: int32 [4, 262144], P(None, 'dom'), may hold values from 0 to 24575, as said below
- interp_weights: float32 [4, 262144], P(None, 'dom'), may hold values from 0.1 to 1
- live_rows: int32 [16], P('dom'), may hold values from 8192 to 16384, as said below
- w_fine: bfloat16 [256, 256], replicated, may hold values from -0.25 to 0.25
- w_parent: bfloat16 [256, 256], replicated, may hold values from -0.25 to 0.25
- w_edge_out: bfloat16 [256, 256], replicated, may hold values from -0.375 to 0.375
- w_node_fine: bfloat16 [256, 256], replicated, may hold values from -0.25 to 0.25
- w_node_agg: bfloat16 [256, 256], replicated, may hold values from -0.25 to 0.25
- w_node_out: bfloat16 [256, 256], replicated, may hold values from -0.375 to 0.375
- edge_bias: float32 [256], replicated, may hold values from -3 to 3
- node_bias: float32 [256], replicated, may hold values from -3 to 3
- norm_gain: float32 [256], replicated, may hold values from 0.1 to 1.9
- norm_bias: float32 [256], replicated, may hold values from -2 to 2
Outputs:
- fine_out: bfloat16 [256, 262144], P('feat', 'dom')
Inputs may be any that keep to these rules, and one draw needn't show every extreme that they name: `parents`: a parent slot s of a fine node of block b names coarse node (b - 1) * 8192 + s, block b holding coarse nodes b * 8192 to (b + 1) * 8192 - 1; slots of block 0 are at least 8192, slots of the last block under 2 * 8192. `live_rows`: fine node slots of a block at or beyond its count are padding; at least one block is full.
All inputs are finite; a program needn't handle non-finite values.
Results may differ from a plain program's by a relative error of at most 0.0042.
Values may be sent and summed in bfloat16 or wider, within the bound.
No kernel may reach another device: no remote copies, remote signals or barrier semaphores. Data moves between devices by JAX's collectives and lax.ppermute only.
A program may use at most 128 MiB of HBM per device.

v0:
```python
import functools

import jax
import jax.numpy as jnp
from jax import lax
from jax.experimental import pallas as pl
from jax.experimental.pallas import tpu as pltpu
from jax.sharding import PartitionSpec as P

F32 = jnp.float32
BF16 = jnp.bfloat16
PAD = 8
CHUNKS = 2
STEP = 256
GROUPS = 16


def dot(a, b, ca, cb):
    return lax.dot_general(a, b, (((ca,), (cb,)), ((), ())), preferred_element_type=F32)


def fill_table(segments, step, places, refs, weight, table, landed, sems):
    rows = (table.shape[0] - 2 * PAD) // 6
    features = landed.shape[2] // sems.shape[2]
    table[pl.ds(0, PAD), :] = jnp.zeros((PAD, 128), F32)
    table[pl.ds(PAD + 6 * rows, PAD), :] = jnp.zeros((PAD, 128), F32)

    def copies(segment, i, slot, which):
        found = []
        for p, (sources, first) in enumerate(segments[segment][3]):
            at = pl.multiple_of(first + i * step, 128)
            found.append(
                pltpu.make_async_copy(
                    refs[sources[min(which, len(sources) - 1)]].at[:, pl.ds(at, step)],
                    landed.at[segment % 2, slot, pl.ds(p * features, features), :],
                    sems.at[segment % 2, slot, p],
                )
            )
        return found

    def start(segment, i, slot):
        if all(len(sources) == 1 for sources, _ in segments[segment][3]):
            for copy in copies(segment, i, slot, 0):
                copy.start()
            return
        for which in range(2):

            @pl.when(places[3] == which)
            def _(which=which):
                for copy in copies(segment, i, slot, which):
                    copy.start()

    start(0, 0, 0)
    for segment, (window, row, length, _) in enumerate(segments):
        steps = length // step
        if segment + 1 < len(segments):
            start(segment + 1, 0, 0)

        def one(i, carry, segment=segment, window=window, row=row, steps=steps):
            slot = lax.rem(i, 2)

            @pl.when(i + 1 < steps)
            def _():
                start(segment, i + 1, 1 - slot)

            for copy in copies(segment, i, slot, 0):
                copy.wait()
            projected = dot(landed[segment % 2, slot], weight[...], 0, 0)
            base = pl.multiple_of(PAD + 2 * (places[window] * rows + row + i * step), 8)
            table[pl.ds(base, step, stride=2), :] = projected[:, :128]
            table[pl.ds(base + 1, step, stride=2), :] = projected[:, 128:]
            return carry

        lax.fori_loop(0, steps, one, 0)


def update_kernel(sources, step, start, segments, table_step, places, aux, *refs):
    count = len(sources)
    given = 1 + max(at for source in sources for at, _ in source)
    arrays, refs = refs[:given], refs[given:]
    scales, w_latent, w_edge, w_agg, w_out_t, bias, gain, shift = refs[:8]
    table, latents, fine, total, earlier, later, scale_rows, slots, live, sems = refs[-10:]
    refs = refs[8:-10]
    features, nodes = latents.shape[0] // count, latents.shape[1]
    parents = slots.shape[0] // nodes
    if segments is None:
        kept, outs = refs[0], refs[1:]
        move = pltpu.make_async_copy(kept, table, sems.at[parents + 1 + count])
        move.start()
    else:
        w_parent, *coarse = refs[: -count - 3]
        *outs, kept, landed, landed_sems = refs[-count - 3 :]
        move = pltpu.make_async_copy(table, kept, sems.at[parents + 1 + count])
    held = aux.shape[0] // (parents + 1)
    fetches = [
        pltpu.make_async_copy(aux.at[pl.ds(k * held + start, nodes)], slots.at[pl.ds(k * nodes, nodes)], sems.at[k])
        for k in range(parents)
    ]
    fetches.append(pltpu.make_async_copy(aux.at[pl.ds(parents * held, 1024)], live, sems.at[parents]))
    for fetch in fetches:
        fetch.start()

    def bring(p, which):
        at, shifted = sources[p][min(which, len(sources[p]) - 1)]
        column = pl.multiple_of(places[4] + start, 128) if shifted else 0
        return pltpu.make_async_copy(
            arrays[at].at[:, pl.ds(column, nodes)],
            latents.at[pl.ds(p * features, features), :],
            sems.at[parents + 1 + p],
        )

    for p, source in enumerate(sources):
        for which in range(len(source)):

            @pl.when((places[3] == which) | (len(source) == 1))
            def _(p=p, which=which):
                bring(p, which).start()

    if segments is not None:
        fill_table(segments, table_step, places, coarse, w_parent, table, landed, landed_sems)
        move.start()
    for fetch in fetches:
        fetch.wait()
    for p in range(count):
        bring(p, 0).wait()
    if segments is None:
        move.wait()
    sublane = lax.broadcasted_iota(jnp.int32, (8, 128), 0)
    owns = [sublane >= 2 * j for j in range(4)]

    def begin(i):
        columns = pl.ds(pl.multiple_of(i * step, step), step)
        first = dot(latents[:, columns], w_latent[...], 0, 0) + bias[...]
        return first, scales[:, pl.ds(pl.multiple_of(start + i * step, step), step)].T

    def keep(first, scale_columns):
        width = first.shape[1] // 2
        fine[pl.ds(0, step, stride=2), :] = first[:, :128]
        fine[pl.ds(1, step, stride=2), :] = first[:, 128:width]
        later[...] = first[:, width:]
        scale_rows[pl.ds(0, step, stride=2), :] = scale_columns
        scale_rows[pl.ds(1, step, stride=2), :] = scale_columns

    def group(at, g):
        part = fine[pl.ds(g * 8, 8), :]
        scale = scale_rows[pl.ds(g * 8, 8), :]
        acc = None
        for k in range(parents):
            rows = None
            for j in range(4):
                loaded = table[pl.ds(slots[at + (k * nodes + g * 4 + j)], 8), :]
                rows = loaded if rows is None else jnp.where(owns[j], loaded, rows)
            hidden = jnp.maximum(part + rows, 0.0) * scale[:, k : k + 1]
            acc = hidden if acc is None else acc + hidden
        return acc

    def finish(i, summed, own_part):
        at = pl.multiple_of(i * step, step)
        aggregate = dot(summed.astype(BF16), w_edge[...], 1, 0).astype(BF16)
        node_hidden = jnp.maximum(own_part + dot(aggregate, w_agg[...], 1, 0), 0.0).astype(BF16)
        output = dot(w_out_t[...], node_hidden, 1, 1)
        centered = output - jnp.mean(output, axis=0, keepdims=True)
        spread = jnp.mean(centered * centered, axis=0, keepdims=True)
        normed = centered * lax.rsqrt(spread + 1e-05) * gain[...] + shift[...]
        column = start + at + lax.broadcasted_iota(jnp.int32, (1, step), 1)
        moved = jnp.where(column < live[0], normed, 0.0)
        return (latents[:, pl.ds(at, step)].astype(F32) + moved).astype(BF16)

    def write(i, result):
        for r in range(count):
            outs[r][:, pl.ds(pl.multiple_of(i * step, step), step)] = result[r * features : (r + 1) * features]

    def gathered():
        return jnp.concatenate([total[pl.ds(0, step, stride=2), :], total[pl.ds(1, step, stride=2), :]], axis=1)

    steps = nodes // step
    keep(*begin(0))

    def one_step(i, carry):
        before, after = jnp.maximum(i - 1, 0), jnp.minimum(i + 1, steps - 1)
        summed, own_part, current = gathered(), earlier[...], later[...]
        result = finish(before, summed, own_part)
        begun = begin(after)
        for first in range(0, step // 4, GROUPS):
            sums = [group(pl.multiple_of(i * step, step), first + g) for g in range(GROUPS)]
            total[pl.ds(first * 8, GROUPS * 8), :] = jnp.concatenate(sums, axis=0)
        write(before, result)
        earlier[...] = current
        keep(*begun)
        return carry

    lax.fori_loop(0, steps, one_step, 0)
    write(steps - 1, finish(steps - 1, gathered(), earlier[...]))
    if segments is not None:
        move.wait()


def update(
    start, nodes, aux, arrays, sources, scales, params, places, table=None, segments=None, w_parent=None, coarse=()
):
    count, features = len(sources), arrays[0].shape[0]
    parents = aux.shape[0] - 1
    step = min(STEP, nodes)
    vmem = pl.BlockSpec(memory_space=pltpu.VMEM)
    smem = pl.BlockSpec(memory_space=pltpu.SMEM)
    far = pl.BlockSpec(memory_space=pltpu.HBM)
    out_shape = [jax.ShapeDtypeStruct((features, nodes), BF16)] * count
    operands = [places, aux.reshape(-1), *arrays, scales, *params]
    specs = [smem, far] + [far] * len(arrays) + [vmem] * (1 + len(params))
    scratch, table_step = [], 0
    if segments is None:
        operands, specs = operands + [table], specs + [far]
    else:
        operands, specs = operands + [w_parent, *coarse], specs + [vmem] + [far] * len(coarse)
        table_step = min(2048, segments[0][2])
        table = jax.ShapeDtypeStruct((2 * sum(segment[2] for segment in segments) + 2 * PAD, 128), F32)
        out_shape.append(table)
        scratch = [
            pltpu.VMEM((2, 2, w_parent.shape[0], table_step), BF16),
            pltpu.SemaphoreType.DMA((2, 2, len(segments[0][3]))),
        ]
    return pl.pallas_call(
        functools.partial(update_kernel, sources, step, start, segments, table_step),
        out_shape=out_shape,
        in_specs=specs,
        out_specs=[vmem] * count + [far] * (len(out_shape) - count),
        scratch_shapes=scratch
        + [
            pltpu.VMEM(table.shape, F32),
            pltpu.VMEM((count * features, nodes), BF16),
            pltpu.VMEM((2 * step, 128), F32),
            pltpu.VMEM((2 * step, 128), F32),
            pltpu.VMEM((step, 256), F32),
            pltpu.VMEM((step, 256), F32),
            pltpu.VMEM((2 * step, 8), F32),
            pltpu.SMEM((parents * nodes,), jnp.int32),
            pltpu.SMEM((1024,), jnp.int32),
            pltpu.SemaphoreType.DMA((parents + 2 + count,)),
        ],
        compiler_params=pltpu.CompilerParams(vmem_limit_bytes=40 << 20),
        cost_estimate=pl.CostEstimate(flops=nodes * 700000, bytes_accessed=nodes * 2048, transcendentals=nodes),
    )(*operands)


def after(value, *others):
    return lax.optimization_barrier((value, *others))[0]


def cut(array, at, size):
    return lax.dynamic_slice_in_dim(array, at, size, 1)


def plain(fine_latent, coarse_latent, aux, weights, w_parent, run):
    groups, domains = lax.axis_size("feat"), lax.axis_size("dom")
    rank = lax.axis_index("feat")
    per_device = fine_latent.shape[1] // groups
    length = per_device // CHUNKS
    forward = [(i, i + 1) for i in range(domains - 1)]
    backward = [(i + 1, i) for i in range(domains - 1)]

    def turn(value, r):
        return lax.ppermute(value, "feat", [(i, (i + r) % groups) for i in range(groups)])

    own = [coarse_latent] + [turn(coarse_latent, r) for r in range(1, groups)]
    low = [lax.ppermute(piece, "dom", forward) for piece in own]
    high = [lax.ppermute(piece, "dom", backward) for piece in own]
    first_row = rank * per_device
    rows = coarse_latent.shape[1]
    segments = [
        (w, 0, rows, [((w * groups + p,), 0) for p in range(groups)]) for w in range(3)
    ]
    making = dict(segments=segments, w_parent=w_parent, coarse=low + own + high)
    places = jnp.stack([0, 1, 2, 0, first_row]).astype(jnp.int32)
    sources = [((0, True),)] + [((r, False),) for r in range(1, groups)]
    aux = cut(aux, first_row, per_device)
    aux = jnp.concatenate([aux[:-1], aux[-1:] - first_row])
    weights = cut(weights, first_row, per_device)
    result = fine_latent
    arrived = []
    for c in range(CHUNKS):
        start = c * length
        pieces = [fine_latent]
        for r in range(1, groups):
            part = cut(fine_latent, ((rank + r) % groups) * per_device + start, length)
            pieces.append(turn(after(part, own[-1]), r))
        outs = run(start, length, aux, pieces, sources, weights, places, **(making if c == 0 else dict(table=table)))
        table = outs[-1] if c == 0 else table
        result = lax.dynamic_update_slice_in_dim(result, outs[0], first_row + start, 1)
        for r in range(1, groups):
            arrived.append((turn(outs[r], -r), ((rank + r) % groups) * per_device + start))
    for part, at in arrived:
        result = lax.dynamic_update_slice_in_dim(result, part, at, 1)
    return result


def paired(fine_latent, coarse_latent, aux, weights, w_parent, run):
    domains = lax.axis_size("dom")
    side, rank = lax.axis_index("dom") % 2, lax.axis_index("feat")
    matched = side == rank
    pairs = range(domains // 2)

    def send(value, moves):
        perm = [((2 * c + a) * 2 + b, (2 * c + x) * 2 + y) for c in pairs for (a, b), (x, y) in moves]
        return lax.ppermute(value, ("dom", "feat"), perm)

    def swap_rank(value):
        return send(value, [((k, f), (k, 1 - f)) for k in range(2) for f in range(2)])

    def swap_side(value):
        return send(value, [((k, f), (1 - k, f)) for k in range(2) for f in range(2)])

    def halo(value):
        perm = [((2 * c - 1) * 2, (2 * c) * 2) for c in pairs if c > 0]
        perm += [((2 * c + 2) * 2 + 1, (2 * c + 1) * 2 + 1) for c in pairs if c + 1 < len(pairs)]
        return lax.ppermute(value, ("dom", "feat"), perm)

    def hand_over(value):
        return send(value, [((0, 0), (1, 0)), ((1, 1), (0, 1))])

    to_first = [((0, 0), (1, 0)), ((1, 1), (0, 1)), ((0, 1), (0, 0)), ((1, 0), (1, 1))]
    from_first = [(b, a) for a, b in to_first]
    to_second = [((0, 1), (1, 0)), ((1, 0), (0, 1))]

    half = fine_latent.shape[1] // 2
    mine = side * half
    rows = coarse_latent.shape[1]
    mate = swap_rank(coarse_latent)
    halo_own, other = halo(coarse_latent), swap_side(after(coarse_latent, mate))
    halo_mate, other_mate = halo(mate), swap_side(mate)
    passed_own, passed_mate = hand_over(halo_own), hand_over(halo_mate)
    coarse = [coarse_latent, mate, other, other_mate, halo_own, passed_own, halo_mate, passed_mate]
    segments = [
        (0, 0, rows, [((0,), 0), ((1,), 0)]),
        (1, 0, rows, [((2,), 0), ((3,), 0)]),
        (2, 0, rows, [((4, 5), 0), ((6, 7), 0)]),
    ]
    places = jnp.stack([side + 1 - rank, 2 - side - rank, 2 * rank, jnp.where(matched, 0, 1), mine])
    places = places.astype(jnp.int32)

    length = half // CHUNKS
    chunks = []
    for c in range(CHUNKS):
        start = c * length
        first = cut(fine_latent, jnp.where(matched, half - mine, mine) + start, length)
        second = cut(fine_latent, half - mine + start, length)
        first, second = send(after(first, mate), to_first), send(after(second, mate), to_second)
        chunks.append([first, fine_latent, second])

    aux_local, aux_sent = cut(aux, mine, half), cut(aux, half - mine, half)
    aux = jnp.where(matched, aux_local, hand_over(aux_sent))
    aux = jnp.concatenate([aux[:-1], aux[-1:] - mine])
    weights = jnp.where(matched, cut(weights, mine, half), hand_over(cut(weights, half - mine, half)))

    making = dict(segments=segments, w_parent=w_parent, coarse=coarse)
    sources = [((0, False),), ((1, True), (2, False))]
    result = jnp.zeros_like(fine_latent)
    moved = []
    for c in range(CHUNKS):
        start = c * length
        out, kept, *made = run(
            start, length, aux, chunks[c], sources, weights, places, **(making if c == 0 else dict(table=table))
        )
        table = made[0] if made else table
        moved.append((start, kept, send(out, from_first), send(kept, to_second)))
    for start, kept, first, second in moved:
        result = lax.dynamic_update_slice_in_dim(result, jnp.where(matched, kept, first), mine + start, 1)
        result = lax.dynamic_update_slice_in_dim(
            result, jnp.where(matched, first, second), half - mine + start, 1
        )
    return result


def shards(
    fine_latent,
    coarse_latent,
    parents,
    interp_weights,
    live_rows,
    w_fine,
    w_parent,
    w_edge_out,
    w_node_fine,
    w_node_agg,
    w_node_out,
    edge_bias,
    node_bias,
    norm_gain,
    norm_bias,
):
    groups, domains = lax.axis_size("feat"), lax.axis_size("dom")
    rank = lax.axis_index("feat")
    own_features = fine_latent.shape[0]
    owners = [(rank - r) % groups for r in range(groups)]
    pairing = groups == 2 and domains % 2 == 0
    flip = jnp.where(lax.axis_index("dom") % 2 == rank, 1, 0) if pairing else 0

    def ordered(weight, axis, flip=flip):
        parts = [lax.dynamic_slice_in_dim(weight, o * own_features, own_features, axis) for o in owners]
        if pairing:
            parts = [jnp.where(flip == 1, parts[1], parts[0]), jnp.where(flip == 1, parts[0], parts[1])]
        return jnp.concatenate(parts, axis=axis)

    params = (
        jnp.concatenate([ordered(w_fine, 0), ordered(w_node_fine, 0)], axis=1),
        w_edge_out,
        w_node_agg,
        ordered(w_node_out, 1).T,
        jnp.concatenate([edge_bias, node_bias])[None],
        jnp.broadcast_to(ordered(norm_gain, 0)[:, None], (norm_gain.shape[0], STEP)),
        jnp.broadcast_to(ordered(norm_bias, 0)[:, None], (norm_bias.shape[0], STEP)),
    )

    def run(start, nodes, aux, arrays, sources, weights, places, **table):
        scales = jnp.pad(weights, ((0, 8 - weights.shape[0]), (0, 0)))
        return update(start, nodes, aux, arrays, sources, scales, params, places, **table)

    count = parents.shape[1]
    slots = 2 * parents + (PAD - 2 * (jnp.arange(count, dtype=jnp.int32) % 4))
    aux = jnp.concatenate([slots, jnp.broadcast_to(live_rows[:, None], (1, count))])
    plan = paired if pairing else plain
    return plan(fine_latent, coarse_latent, aux, interp_weights, ordered(w_parent, 0, 0), run)


def solution(mesh):
    in_specs = (P("feat", "dom"), P("feat", "dom"), P(None, "dom"), P(None, "dom"), P("dom")) + (P(),) * 10
    return jax.shard_map(shards, mesh=mesh, in_specs=in_specs, out_specs=P("feat", "dom"), check_vma=False)
```

profile of v0, /device:TPU:1, one launch (start us, length us, event | category | flops | bytes accessed | tf_op | source)
XLA Modules:
  0.0 187.2 jit_solution(6782456576890112632)
XLA Ops:
  0.0 2.1 %collective-permute-start.1 = (bf16[128,8192]{1,0:T(8,128)(2,1)}, bf16[128,8192]{1,0:T(8,128)(2,1)}, u32[]{:S(2)}, u32[]{:S(2)}) collective-permute-start(bf16[128,8192]{1,0:T(8,128)(2,1)} %refs_12_.1), channel_id=1, source_target_pairs={{0,1},{1,0},{2,3},{3,2},{4,5},{5,4},{6,7},{7,6},{8,9},{9,8},{10,11... | collective-permute-start | bytes 6291464 | tf_op jit(solution)/shard_map/ppermute | solution.py:304
  2.1 5.3 %collective-permute-start.7 = (bf16[128,8192]{1,0:T(8,128)(2,1)}, bf16[128,8192]{1,0:T(8,128)(2,1)}, u32[]{:S(2)}, u32[]{:S(2)}) collective-permute-start(bf16[128,8192]{1,0:T(8,128)(2,1)} %refs_12_.1), channel_id=1, source_target_pairs={{2,4},{6,8},{10,12},{14,16},{18,20},{22,24},{26,28},{5,3},{9,7},{1... | collective-permute-start | bytes 6291464 | tf_op jit(solution)/shard_map/ppermute | solution.py:315
  8.1 1.0 multiply_add_fusion
  9.1 1.3 collective-permute-start
  10.4 1.6 constant_dynamic-slice_fusion.6
  12.0 1.3 collective-permute-start.4
  13.4 0.9 constant_dynamic-slice_fusion.5
  14.2 0.1 copy.18
  14.5 0.8 broadcast_select_fusion.7
  15.4 0.7 pad_maximum_fusion.1
  16.1 0.9 constant_dynamic-slice_fusion.3
  17.0 0.7 pad_maximum_fusion.refs_11_
  17.6 1.7 broadcast_select_fusion.3
  19.3 4.4 %constant_dynamic-slice_fusion = (bf16[128,4096]{1,0:T(8,128)(2,1)}, bf16[128,4096]{1,0:T(8,128)(2,1)}, bf16[128,4096]{1,0:T(8,128)(2,1)}, bf16[128,4096]{1,0:T(8,128)(2,1)}) fusion(bf16[128,16384]{1,0:T(8,128)(2,1)} %refs_1_.3, s32[]{:T(128)S(6)} %select_n.205, s32[]{:T(128)S(6)} %select_n.204, s32[]{:T(128)S(6)} %select_n.178, s32[]{:T(128)S(6)} %select_n.181), kind=kLoop, calls=%fused_computation.27 | loop fusion | bytes 8388624 | tf_op jit(solution)/shard_map/dynamic_slice | solution.py:250
  23.9 1.0 maximum_maximum_fusion.refs_4_
  24.8 22.9 %collective-permute-done.1.refs_13_ = bf16[128,8192]{1,0:T(8,128)(2,1)} collective-permute-done((bf16[128,8192]{1,0:T(8,128)(2,1)}, bf16[128,8192]{1,0:T(8,128)(2,1)}, u32[]{:S(2)}, u32[]{:S(2)}) %collective-permute-start.1) | collective-permute-done | bytes 2097184 | tf_op jit(solution)/shard_map/ppermute | solution.py:304
  47.7 5.8 %collective-permute-start.9 = (bf16[128,8192]{1,0:T(8,128)(2,1)}, bf16[128,8192]{1,0:T(8,128)(2,1)}, u32[]{:S(2)}, u32[]{:S(2)}) collective-permute-start(bf16[128,8192]{1,0:T(8,128)(2,1)} %collective-permute-done.1.refs_13_), channel_id=1, source_target_pairs={{2,4},{6,8},{10,12},{14,16},{18,20},{22,24},{26,28},{5,3},{9,7},{1... | collective-permute-start | bytes 6291464 | tf_op jit(solution)/shard_map/ppermute | solution.py:315
  53.5 0.9 dynamic-slice_select_fusion
  54.6 1.9 %collective-permute-start.3 = (bf16[128,4096]{1,0:T(8,128)(2,1)}, bf16[128,4096]{1,0:T(8,128)(2,1)}, u32[]{:S(2)}, u32[]{:S(2)}) collective-permute-start(bf16[128,4096]{1,0:T(8,128)(2,1)} %get-tuple-element.16), channel_id=1, source_target_pairs={{1,2},{2,1},{5,6},{6,5},{9,10},{10,9},{13,14},{14,13},{17,18},{18,... | collective-permute-start | bytes 3145736 | tf_op jit(solution)/shard_map/ppermute | solution.py:304
  56.5 0.2 collective-permute-start.5
  56.7 0.3 collective-permute-start.6
  57.1 9.5 %collective-permute-done.2.refs_0_ = bf16[128,4096]{1,0:T(8,128)(2,1)S(1)} collective-permute-done((bf16[128,4096]{1,0:T(8,128)(2,1)}, bf16[128,4096]{1,0:T(8,128)(2,1)S(1)}, u32[]{:S(2)}, u32[]{:S(2)}) %collective-permute-start.2) | collective-permute-done | bytes 1048608 | tf_op jit(solution)/shard_map/ppermute | solution.py:304
  66.6 1.0 copy-done.2
  67.5 1.3 collective-permute-start.8
  68.8 6.6 %collective-permute-done.9.refs_18_ = bf16[128,8192]{1,0:T(8,128)(2,1)} collective-permute-done((bf16[128,8192]{1,0:T(8,128)(2,1)}, bf16[128,8192]{1,0:T(8,128)(2,1)}, u32[]{:S(2)}, u32[]{:S(2)}) %collective-permute-start.9) | collective-permute-done | bytes 2097184 | tf_op jit(solution)/shard_map/ppermute | solution.py:315
  75.5 1.3 collective-permute-start.10
  77.0 0.8 collective-permute-done.3.refs_2_
  77.8 2.2 %collective-permute-start.13 = (bf16[128,4096]{1,0:T(8,128)(2,1)}, bf16[128,4096]{1,0:T(8,128)(2,1)}, u32[]{:S(2)}, u32[]{:S(2)}) collective-permute-start(bf16[128,4096]{1,0:T(8,128)(2,1)} %get-tuple-element.20), channel_id=1, source_target_pairs={{0,2},{3,1},{1,0},{2,3},{4,6},{7,5},{5,4},{6,7},{8,10},{11,9},{9,8... | collective-permute-start | bytes 3145736 | tf_op jit(solution)/shard_map/ppermute | solution.py:304
  80.0 3.0 %collective-permute-start.14 = (bf16[128,4096]{1,0:T(8,128)(2,1)}, bf16[128,4096]{1,0:T(8,128)(2,1)}, u32[]{:S(2)}, u32[]{:S(2)}) collective-permute-start(bf16[128,4096]{1,0:T(8,128)(2,1)} %get-tuple-element.21), channel_id=1, source_target_pairs={{1,2},{2,1},{5,6},{6,5},{9,10},{10,9},{13,14},{14,13},{17,18},{18,... | collective-permute-start | bytes 3145736 | tf_op jit(solution)/shard_map/ppermute | solution.py:304
  83.2 1.2 copy-done.3
  84.4 0.9 copy-done.6
  85.3 0.9 copy-done.8
  86.2 0.9 copy-done.10
  87.1 35.0 %shard_map.145 = (bf16[128,4096]{1,0:T(8,128)(2,1)}, bf16[128,4096]{1,0:T(8,128)(2,1)S(1)}, f32[49168,128]{1,0:T(8,128)}) custom-call(s32[5]{0:T(128)S(1)} %stack.23.places, s32[40960]{0:T(1024)S(1)} %reshape.20.aux, bf16[128,4096]{1,0:T(8,128)(2,1)S(1)} %copy-done.3, bf16[128,16384]{1,0:T(8,128)(2,1)} %refs_1_.3, ...), custom_call_target="tpu_custom_call" | custom-call | flops 2867200000 | bytes 8388608 | tf_op jit(solution)/shard_map/pallas_call | solution.py:222
  122.1 1.0 copy-done.4
  123.1 2.6 %collective-permute-start.12 = (bf16[128,4096]{1,0:T(8,128)(2,1)}, bf16[128,4096]{1,0:T(8,128)(2,1)S(1)}, u32[]{:S(2)}, u32[]{:S(2)}) collective-permute-start(bf16[128,4096]{1,0:T(8,128)(2,1)} %copy-done.4), channel_id=1, source_target_pairs={{1,2},{2,1},{5,6},{6,5},{9,10},{10,9},{13,14},{14,13},{17,18},{18,... | collective-permute-start | bytes 3145736 | tf_op jit(solution)/shard_map/ppermute | solution.py:304
  125.7 2.2 %copy-done = bf16[128,16384]{1,0:T(8,128)(2,1)S(1)} copy-done((bf16[128,16384]{1,0:T(8,128)(2,1)S(1)}, bf16[128,16384]{1,0:T(8,128)(2,1)}, u32[]{:S(2)}) %copy-start) | copy-done | bytes 4194328
  127.9 0.9 copy-done.7
  128.8 0.9 copy-done.9
  129.7 31.3 %shard_map.146 = (bf16[128,4096]{1,0:T(8,128)(2,1)S(1)}, bf16[128,4096]{1,0:T(8,128)(2,1)S(1)}) custom-call(s32[5]{0:T(128)S(1)} %stack.23.places, s32[40960]{0:T(1024)S(1)} %reshape.20.aux, bf16[128,4096]{1,0:T(8,128)(2,1)} %collective-permute-done.13.refs_0_, bf16[128,16384]{1,0:T(8,128)(2,1)S(1)} %copy-done, ...), custom_call_target="tpu_custom_call" | custom-call | flops 2867200000 | bytes 8388608 | tf_op jit(solution)/shard_map/pallas_call | solution.py:222
  161.1 3.1 %collective-permute-start.16 = (bf16[128,4096]{1,0:T(8,128)(2,1)S(1)}, bf16[128,4096]{1,0:T(8,128)(2,1)S(1)}, u32[]{:S(2)}, u32[]{:S(2)}) collective-permute-start(bf16[128,4096]{1,0:T(8,128)(2,1)S(1)} %get-tuple-element.23), channel_id=1, source_target_pairs={{1,2},{2,1},{5,6},{6,5},{9,10},{10,9},{13,14},{14,13},{17,18},{18,... | collective-permute-start | bytes 3145736 | tf_op jit(solution)/shard_map/ppermute | solution.py:304
  164.2 0.4 broadcast_in_dim.10
  164.6 1.5 select_dynamic-update-slice_fusion.3
  166.2 0.3 select_dynamic-update-slice_fusion.2
  166.5 16.8 %collective-permute-done.15 = bf16[128,4096]{1,0:T(8,128)(2,1)S(1)} collective-permute-done((bf16[128,4096]{1,0:T(8,128)(2,1)S(1)}, bf16[128,4096]{1,0:T(8,128)(2,1)S(1)}, u32[]{:S(2)}, u32[]{:S(2)}) %collective-permute-start.15) | collective-permute-done | bytes 1048608 | tf_op jit(solution)/shard_map/ppermute | solution.py:304
  183.3 0.3 select_dynamic-update-slice_fusion.1
  183.6 2.4 %collective-permute-done.16 = bf16[128,4096]{1,0:T(8,128)(2,1)S(1)} collective-permute-done((bf16[128,4096]{1,0:T(8,128)(2,1)S(1)}, bf16[128,4096]{1,0:T(8,128)(2,1)S(1)}, u32[]{:S(2)}, u32[]{:S(2)}) %collective-permute-start.16) | collective-permute-done | bytes 1048608 | tf_op jit(solution)/shard_map/ppermute | solution.py:304
  186.0 1.2 select_dynamic-update-slice_fusion
  (47 shorter events, 0.8 us)
Async XLA Ops:
  0.0 47.7 %collective-permute-start.1 = (bf16[128,8192]{1,0:T(8,128)(2,1)}, bf16[128,8192]{1,0:T(8,128)(2,1)}, u32[]{:S(2)}, u32[]{:S(2)}) collective-permute-start(bf16[128,8192]{1,0:T(8,128)(2,1)} %refs_12_.1), channel_id=1, source_target_pairs={{0,1},{1,0},{2,3},{3,2},{4,5},{5,4},{6,7},{7,6},{8,9},{9,8},{10,11... | collective-permute-start | bytes 6291464 | tf_op jit(solution)/shard_map/ppermute | solution.py:304
  2.1 54.7 %collective-permute-start.7 = (bf16[128,8192]{1,0:T(8,128)(2,1)}, bf16[128,8192]{1,0:T(8,128)(2,1)}, u32[]{:S(2)}, u32[]{:S(2)}) collective-permute-start(bf16[128,8192]{1,0:T(8,128)(2,1)} %refs_12_.1), channel_id=1, source_target_pairs={{2,4},{6,8},{10,12},{14,16},{18,20},{22,24},{26,28},{5,3},{9,7},{1... | collective-permute-start | bytes 6291464 | tf_op jit(solution)/shard_map/ppermute | solution.py:315
  9.1 45.4 %collective-permute-start = (s32[5,8192]{1,0:T(8,128)S(1)}, s32[5,8192]{1,0:T(8,128)S(1)}, u32[]{:S(2)}, u32[]{:S(2)}) collective-permute-start(s32[5,8192]{1,0:T(8,128)S(1)} %pad_dynamic-slice_fusion), channel_id=1, source_target_pairs={{0,2},{3,1},{4,6},{7,5},{8,10},{11,9},{12,14},{15,13},{16,18},{19,... | collective-permute-start | bytes 491528 | tf_op jit(solution)/shard_map/ppermute | solution.py:304
  12.0 41.5 %collective-permute-start.4 = (f32[4,8192]{1,0:T(4,128)}, f32[4,8192]{1,0:T(4,128)}, u32[]{:S(2)}, u32[]{:S(2)}) collective-permute-start(f32[4,8192]{1,0:T(4,128)} %constant_dynamic-slice_fusion.6), channel_id=1, source_target_pairs={{0,2},{3,1},{4,6},{7,5},{8,10},{11,9},{12,14},{15,13},{16,18},{19,... | collective-permute-start | bytes 393224 | tf_op jit(solution)/shard_map/ppermute | solution.py:304
  19.3 34.2 %copy-start.12 = (f32[4,16384]{1,0:T(4,128)S(1)}, f32[4,16384]{1,0:T(4,128)}, u32[]{:S(2)}) copy-start(f32[4,16384]{1,0:T(4,128)} %param.18) | copy-start | bytes 786436
  19.3 37.2 %copy-start.1 = (bf16[128,8192]{1,0:T(8,128)(2,1)S(1)}, bf16[128,8192]{1,0:T(8,128)(2,1)}, u32[]{:S(2)}) copy-start(bf16[128,8192]{1,0:T(8,128)(2,1)} %refs_12_.1) | copy-start | bytes 6291460
  47.7 27.7 %collective-permute-start.9 = (bf16[128,8192]{1,0:T(8,128)(2,1)}, bf16[128,8192]{1,0:T(8,128)(2,1)}, u32[]{:S(2)}, u32[]{:S(2)}) collective-permute-start(bf16[128,8192]{1,0:T(8,128)(2,1)} %collective-permute-done.1.refs_13_), channel_id=1, source_target_pairs={{2,4},{6,8},{10,12},{14,16},{18,20},{22,24},{26,28},{5,3},{9,7},{1... | collective-permute-start | bytes 6291464 | tf_op jit(solution)/shard_map/ppermute | solution.py:315
  54.5 12.1 %collective-permute-start.2 = (bf16[128,4096]{1,0:T(8,128)(2,1)}, bf16[128,4096]{1,0:T(8,128)(2,1)S(1)}, u32[]{:S(2)}, u32[]{:S(2)}) collective-permute-start(bf16[128,4096]{1,0:T(8,128)(2,1)} %get-tuple-element.15), channel_id=1, source_target_pairs={{0,2},{3,1},{1,0},{2,3},{4,6},{7,5},{5,4},{6,7},{8,10},{11,9},{9,8... | collective-permute-start | bytes 3145736 | tf_op jit(solution)/shard_map/ppermute | solution.py:304
  54.6 23.2 %collective-permute-start.3 = (bf16[128,4096]{1,0:T(8,128)(2,1)}, bf16[128,4096]{1,0:T(8,128)(2,1)}, u32[]{:S(2)}, u32[]{:S(2)}) collective-permute-start(bf16[128,4096]{1,0:T(8,128)(2,1)} %get-tuple-element.16), channel_id=1, source_target_pairs={{1,2},{2,1},{5,6},{6,5},{9,10},{10,9},{13,14},{14,13},{17,18},{18,... | collective-permute-start | bytes 3145736 | tf_op jit(solution)/shard_map/ppermute | solution.py:304
  56.5 23.5 %collective-permute-start.5 = (bf16[128,8192]{1,0:T(8,128)(2,1)S(1)}, bf16[128,8192]{1,0:T(8,128)(2,1)}, u32[]{:S(2)}, u32[]{:S(2)}) collective-permute-start(bf16[128,8192]{1,0:T(8,128)(2,1)S(1)} %copy-done.1), channel_id=1, source_target_pairs={{0,2},{1,3},{2,0},{3,1},{4,6},{5,7},{6,4},{7,5},{8,10},{9,11},{10,... | collective-permute-start | bytes 6291464 | tf_op jit(solution)/shard_map/ppermute | solution.py:304
  56.7 26.2 %collective-permute-start.6 = (bf16[128,8192]{1,0:T(8,128)(2,1)}, bf16[128,8192]{1,0:T(8,128)(2,1)}, u32[]{:S(2)}, u32[]{:S(2)}) collective-permute-start(bf16[128,8192]{1,0:T(8,128)(2,1)} %collective-permute-done.1.refs_13_), channel_id=1, source_target_pairs={{0,2},{1,3},{2,0},{3,1},{4,6},{5,7},{6,4},{7,5},{8,10},{9,11},{10,... | collective-permute-start | bytes 6291464 | tf_op jit(solution)/shard_map/ppermute | solution.py:304
  66.6 1.0 copy-start.2
  67.5 15.5 %collective-permute-start.8 = (bf16[128,8192]{1,0:T(8,128)(2,1)}, bf16[128,8192]{1,0:T(8,128)(2,1)}, u32[]{:S(2)}, u32[]{:S(2)}) collective-permute-start(bf16[128,8192]{1,0:T(8,128)(2,1)} %collective-permute-done.7.refs_16_), channel_id=1, source_target_pairs={{0,2},{3,1},{4,6},{7,5},{8,10},{11,9},{12,14},{15,13},{16,18},{19,... | collective-permute-start | bytes 6291464 | tf_op jit(solution)/shard_map/ppermute | solution.py:304
  75.5 7.5 %collective-permute-start.10 = (bf16[128,8192]{1,0:T(8,128)(2,1)}, bf16[128,8192]{1,0:T(8,128)(2,1)}, u32[]{:S(2)}, u32[]{:S(2)}) collective-permute-start(bf16[128,8192]{1,0:T(8,128)(2,1)} %collective-permute-done.9.refs_18_), channel_id=1, source_target_pairs={{0,2},{3,1},{4,6},{7,5},{8,10},{11,9},{12,14},{15,13},{16,18},{19,... | collective-permute-start | bytes 6291464 | tf_op jit(solution)/shard_map/ppermute | solution.py:304
  77.8 47.9 %collective-permute-start.13 = (bf16[128,4096]{1,0:T(8,128)(2,1)}, bf16[128,4096]{1,0:T(8,128)(2,1)}, u32[]{:S(2)}, u32[]{:S(2)}) collective-permute-start(bf16[128,4096]{1,0:T(8,128)(2,1)} %get-tuple-element.20), channel_id=1, source_target_pairs={{0,2},{3,1},{1,0},{2,3},{4,6},{7,5},{5,4},{6,7},{8,10},{11,9},{9,8... | collective-permute-start | bytes 3145736 | tf_op jit(solution)/shard_map/ppermute | solution.py:304
  80.0 45.8 %collective-permute-start.14 = (bf16[128,4096]{1,0:T(8,128)(2,1)}, bf16[128,4096]{1,0:T(8,128)(2,1)}, u32[]{:S(2)}, u32[]{:S(2)}) collective-permute-start(bf16[128,4096]{1,0:T(8,128)(2,1)} %get-tuple-element.21), channel_id=1, source_target_pairs={{1,2},{2,1},{5,6},{6,5},{9,10},{10,9},{13,14},{14,13},{17,18},{18,... | collective-permute-start | bytes 3145736 | tf_op jit(solution)/shard_map/ppermute | solution.py:304
  83.2 1.2 copy-start.3
  84.4 0.9 copy-start.6
  85.3 0.9 copy-start.8
  86.2 0.9 copy-start.10
  122.1 1.0 copy-start.4
  123.1 41.1 %collective-permute-start.11 = (bf16[128,4096]{1,0:T(8,128)(2,1)}, bf16[128,4096]{1,0:T(8,128)(2,1)}, u32[]{:S(2)}, u32[]{:S(2)}) collective-permute-start(bf16[128,4096]{1,0:T(8,128)(2,1)} %get-tuple-element.19), channel_id=1, source_target_pairs={{2,0},{1,3},{0,1},{3,2},{6,4},{5,7},{4,5},{7,6},{10,8},{9,11},{8,9... | collective-permute-start | bytes 3145736 | tf_op jit(solution)/shard_map/ppermute | solution.py:304
  123.1 43.1 %collective-permute-start.12 = (bf16[128,4096]{1,0:T(8,128)(2,1)}, bf16[128,4096]{1,0:T(8,128)(2,1)S(1)}, u32[]{:S(2)}, u32[]{:S(2)}) collective-permute-start(bf16[128,4096]{1,0:T(8,128)(2,1)} %copy-done.4), channel_id=1, source_target_pairs={{1,2},{2,1},{5,6},{6,5},{9,10},{10,9},{13,14},{14,13},{17,18},{18,... | collective-permute-start | bytes 3145736 | tf_op jit(solution)/shard_map/ppermute | solution.py:304
  125.7 2.2 %copy-start = (bf16[128,16384]{1,0:T(8,128)(2,1)S(1)}, bf16[128,16384]{1,0:T(8,128)(2,1)}, u32[]{:S(2)}) copy-start(bf16[128,16384]{1,0:T(8,128)(2,1)} %refs_1_.3) | copy-start | bytes 12582916
  127.9 0.9 copy-start.7
  128.8 0.9 copy-start.9
  161.0 3.6 %copy-start.5 = (bf16[128,4096]{1,0:T(8,128)(2,1)S(1)}, bf16[128,4096]{1,0:T(8,128)(2,1)}, u32[]{:S(2)}) copy-start(bf16[128,4096]{1,0:T(8,128)(2,1)} %copy-done.4) | copy-start | bytes 3145732
  161.1 22.2 %collective-permute-start.15 = (bf16[128,4096]{1,0:T(8,128)(2,1)S(1)}, bf16[128,4096]{1,0:T(8,128)(2,1)S(1)}, u32[]{:S(2)}, u32[]{:S(2)}) collective-permute-start(bf16[128,4096]{1,0:T(8,128)(2,1)S(1)} %get-tuple-element.24), channel_id=1, source_target_pairs={{2,0},{1,3},{0,1},{3,2},{6,4},{5,7},{4,5},{7,6},{10,8},{9,11},{8,9... | collective-permute-start | bytes 3145736 | tf_op jit(solution)/shard_map/ppermute | solution.py:304
  161.1 24.9 %collective-permute-start.16 = (bf16[128,4096]{1,0:T(8,128)(2,1)S(1)}, bf16[128,4096]{1,0:T(8,128)(2,1)S(1)}, u32[]{:S(2)}, u32[]{:S(2)}) collective-permute-start(bf16[128,4096]{1,0:T(8,128)(2,1)S(1)} %get-tuple-element.23), channel_id=1, source_target_pairs={{1,2},{2,1},{5,6},{6,5},{9,10},{10,9},{13,14},{14,13},{17,18},{18,... | collective-permute-start | bytes 3145736 | tf_op jit(solution)/shard_map/ppermute | solution.py:304
  183.6 2.4 %copy-start.11 = (bf16[128,16384]{1,0:T(8,128)(2,1)}, bf16[128,16384]{1,0:T(8,128)(2,1)S(1)}, u32[]{:S(2)}) copy-start(bf16[128,16384]{1,0:T(8,128)(2,1)S(1)} %select_dynamic-update-slice_fusion.1) | copy-start | bytes 12582916
where the time goes:
time: 190 us; the launch traced here: 187 us
  Pallas kernels  66.3 us (35%)
  waiting for transfers between devices  59 us (31%)
  starting transfers between devices  31.7 us (17%)
  local copies, waits for them, and re-layouts  18.7 us (10%)
  other arithmetic  10.3 us (5%)
    pallas_call x2, Pallas kernels, update(): pl.pallas_call(functools.partial(update_kernel, sources, step, start, seg...  66.3 us
    ppermute x15, waiting for transfers between devices, send(): return lax.ppermute(value, ('dom', 'feat'), perm)  52.4 us
    ppermute x15, starting transfers between devices, send(): return lax.ppermute(value, ('dom', 'feat'), perm)  20.6 us
    ppermute x2, starting transfers between devices, halo(): return lax.ppermute(value, ('dom', 'feat'), perm)  11.1 us
    unnamed x28, local copies, waits for them, and re-layouts  10.1 us
    ppermute x2, waiting for transfers between devices, halo(): return lax.ppermute(value, ('dom', 'feat'), perm)  6.65 us
    dynamic_slice x3, local copies, waits for them, and re-layouts, cut(): return lax.dynamic_slice_in_dim(array, at, size, 1)  6.02 us
  transfers between devices with their start and end apart: 17, of which 6 were waited for; matrix products, arithmetic and copies ran while one was open for 10% of the time, Pallas kernels for 35%

commit v1 on v0

--- a/solution.py
+++ b/solution.py
@@ -12,7 +12,7 @@
 PAD = 8
 CHUNKS = 2
 STEP = 256
-GROUPS = 16
+GROUPS = 13
 
 
 def dot(a, b, ca, cb):
@@ -93,8 +93,7 @@
         move = pltpu.make_async_copy(table, kept, sems.at[parents + 1 + count])
     held = aux.shape[0] // (parents + 1)
     fetches = [
-        pltpu.make_async_copy(aux.at[pl.ds(k * held + start, nodes)], slots.at[pl.ds(k * nodes, nodes)], sems.at[k])
-        for k in range(parents)
+        pltpu.make_async_copy(aux.at[pl.ds(parents * start, parents * nodes)], slots, sems.at[0]),
     ]
     fetches.append(pltpu.make_async_copy(aux.at[pl.ds(parents * held, 1024)], live, sems.at[parents]))
     for fetch in fetches:
@@ -148,7 +147,7 @@
         for k in range(parents):
             rows = None
             for j in range(4):
-                loaded = table[pl.ds(slots[at + (k * nodes + g * 4 + j)], 8), :]
+                loaded = table[pl.ds(slots[at + (k * step + g * 4 + j)], 8), :]
                 rows = loaded if rows is None else jnp.where(owns[j], loaded, rows)
             hidden = jnp.maximum(part + rows, 0.0) * scale[:, k : k + 1]
             acc = hidden if acc is None else acc + hidden
@@ -157,14 +156,23 @@
     def finish(i, summed, own_part):
         at = pl.multiple_of(i * step, step)
         aggregate = dot(summed.astype(BF16), w_edge[...], 1, 0).astype(BF16)
+        yield
         node_hidden = jnp.maximum(own_part + dot(aggregate, w_agg[...], 1, 0), 0.0).astype(BF16)
+        yield
         output = dot(w_out_t[...], node_hidden, 1, 1)
+        yield
         centered = output - jnp.mean(output, axis=0, keepdims=True)
         spread = jnp.mean(centered * centered, axis=0, keepdims=True)
+        yield
         normed = centered * lax.rsqrt(spread + 1e-05) * gain[...] + shift[...]
         column = start + at + lax.broadcasted_iota(jnp.int32, (1, step), 1)
         moved = jnp.where(column < live[0], normed, 0.0)
-        return (latents[:, pl.ds(at, step)].astype(F32) + moved).astype(BF16)
+        yield (latents[:, pl.ds(at, step)].astype(F32) + moved).astype(BF16)
+
+    def last(parts):
+        for value in parts:
+            pass
+        return value
 
     def write(i, result):
         for r in range(count):
@@ -179,20 +187,27 @@
     def one_step(i, carry):
         before, after = jnp.maximum(i - 1, 0), jnp.minimum(i + 1, steps - 1)
         summed, own_part, current = gathered(), earlier[...], later[...]
-        result = finish(before, summed, own_part)
+        parts = finish(before, summed, own_part)
+        base = pl.multiple_of(i * (parents * step), parents * step)
         begun = begin(after)
         for first in range(0, step // 4, GROUPS):
-            sums = [group(pl.multiple_of(i * step, step), first + g) for g in range(GROUPS)]
-            total[pl.ds(first * 8, GROUPS * 8), :] = jnp.concatenate(sums, axis=0)
+            result = next(parts, None) if first < 4 * GROUPS else last(parts)
+            sums = [group(base, g) for g in range(first, min(first + GROUPS, step // 4))]
+            total[pl.ds(first * 8, len(sums) * 8), :] = jnp.concatenate(sums, axis=0)
         write(before, result)
         earlier[...] = current
         keep(*begun)
         return carry
 
     lax.fori_loop(0, steps, one_step, 0)
-    write(steps - 1, finish(steps - 1, gathered(), earlier[...]))
+    write(steps - 1, last(finish(steps - 1, gathered(), earlier[...])))
     if segments is not None:
         move.wait()
+
+
+def by_step(aux, step):
+    slots = aux[:-1].reshape(aux.shape[0] - 1, -1, step).transpose(1, 0, 2)
+    return jnp.concatenate([slots.reshape(-1), aux[-1]])
 
 
 def update(
@@ -205,7 +220,7 @@
     smem = pl.BlockSpec(memory_space=pltpu.SMEM)
     far = pl.BlockSpec(memory_space=pltpu.HBM)
     out_shape = [jax.ShapeDtypeStruct((features, nodes), BF16)] * count
-    operands = [places, aux.reshape(-1), *arrays, scales, *params]
+    operands = [places, by_step(aux, step), *arrays, scales, *params]
     specs = [smem, far] + [far] * len(arrays) + [vmem] * (1 + len(params))
     scratch, table_step = [], 0
     if segments is None:

time: 190 us -> 187 us (0.984)
  Pallas kernels: 66.3 us -> 64.3 us
    ppermute x2, waiting for transfers between devices: 6.65 us -> 8.77 us  [halo(): return lax.ppermute(value, ('dom', 'feat'), perm)]
    pallas_call x2, Pallas kernels: 66.3 us -> 64.3 us  [update(): pl.pallas_call(functools.partial(update_kernel, sources, step, start, seg...]
    unnamed x28 -> x31, local copies, waits for them, and re-layouts: 10.1 us -> 9.75 us
  transfers between devices with their start and end apart: 17 -> 17, of which waited for: 6 -> 5; matrix products, arithmetic and copies ran while one was open for 10% -> 10% of each run, Pallas kernels for 35% -> 35%
where the time goes in v1:
time: 187 us; the launch traced here: 184 us
  Pallas kernels  64.3 us (34%)
  waiting for transfers between devices  60.3 us (32%)
  starting transfers between devices  30.1 us (16%)
  local copies, waits for them, and re-layouts  18.3 us (10%)
  other arithmetic  10.3 us (6%)
    pallas_call x2, Pallas kernels, update(): pl.pallas_call(functools.partial(update_kernel, sources, step, start, seg...  64.3 us
    ppermute x15, waiting for transfers between devices, send(): return lax.ppermute(value, ('dom', 'feat'), perm)  51.5 us
    ppermute x15, starting transfers between devices, send(): return lax.ppermute(value, ('dom', 'feat'), perm)  20.2 us
    ppermute x2, starting transfers between devices, halo(): return lax.ppermute(value, ('dom', 'feat'), perm)  9.9 us
    unnamed x31, local copies, waits for them, and re-layouts  9.75 us
    ppermute x2, waiting for transfers between devices, halo(): return lax.ppermute(value, ('dom', 'feat'), perm)  8.77 us
    dynamic_slice x3, local copies, waits for them, and re-layouts, cut(): return lax.dynamic_slice_in_dim(array, at, size, 1)  6.03 us
  transfers between devices with their start and end apart: 17, of which 5 were waited for; matrix products, arithmetic and copies ran while one was open for 10% of the time, Pallas kernels for 35%

profile of v1, /device:TPU:1, one launch (start us, length us, event | category | flops | bytes accessed | tf_op | source)
XLA Modules:
  0.0 184.5 jit_solution(14124109452600148300)
XLA Ops:
  0.0 2.1 %collective-permute-start.1 = (bf16[128,8192]{1,0:T(8,128)(2,1)}, bf16[128,8192]{1,0:T(8,128)(2,1)}, u32[]{:S(2)}, u32[]{:S(2)}) collective-permute-start(bf16[128,8192]{1,0:T(8,128)(2,1)} %refs_12_.1), channel_id=1, source_target_pairs={{0,1},{1,0},{2,3},{3,2},{4,5},{5,4},{6,7},{7,6},{8,9},{9,8},{10,11... | collective-permute-start | bytes 6291464 | tf_op jit(solution)/shard_map/ppermute | solution.py:319
  2.1 5.3 %collective-permute-start.7 = (bf16[128,8192]{1,0:T(8,128)(2,1)}, bf16[128,8192]{1,0:T(8,128)(2,1)}, u32[]{:S(2)}, u32[]{:S(2)}) collective-permute-start(bf16[128,8192]{1,0:T(8,128)(2,1)} %refs_12_.1), channel_id=1, source_target_pairs={{2,4},{6,8},{10,12},{14,16},{18,20},{22,24},{26,28},{5,3},{9,7},{1... | collective-permute-start | bytes 6291464 | tf_op jit(solution)/shard_map/ppermute | solution.py:330
  8.1 1.0 multiply_add_fusion
  9.2 1.3 collective-permute-start
  10.5 1.6 constant_dynamic-slice_fusion.6
  12.0 1.3 collective-permute-start.4
  13.4 0.9 constant_dynamic-slice_fusion.5
  14.3 0.1 copy.21
  14.4 0.1 copy.22
  14.5 0.8 broadcast_select_fusion.7
  15.4 0.7 pad_maximum_fusion.1
  16.1 0.9 constant_dynamic-slice_fusion.3
  17.0 0.7 pad_maximum_fusion.refs_11_
  17.7 1.6 broadcast_select_fusion.3
  19.3 4.4 %constant_dynamic-slice_fusion = (bf16[128,4096]{1,0:T(8,128)(2,1)}, bf16[128,4096]{1,0:T(8,128)(2,1)}, bf16[128,4096]{1,0:T(8,128)(2,1)}, bf16[128,4096]{1,0:T(8,128)(2,1)}) fusion(bf16[128,16384]{1,0:T(8,128)(2,1)} %refs_1_.3, s32[]{:T(128)S(6)} %select_n.205, s32[]{:T(128)S(6)} %select_n.204, s32[]{:T(128)S(6)} %select_n.178, s32[]{:T(128)S(6)} %select_n.181), kind=kLoop, calls=%fused_computation.27 | loop fusion | bytes 8388624 | tf_op jit(solution)/shard_map/dynamic_slice | solution.py:265
  23.9 1.0 maximum_maximum_fusion.refs_4_
  24.8 22.9 %collective-permute-done.1.refs_13_ = bf16[128,8192]{1,0:T(8,128)(2,1)} collective-permute-done((bf16[128,8192]{1,0:T(8,128)(2,1)}, bf16[128,8192]{1,0:T(8,128)(2,1)}, u32[]{:S(2)}, u32[]{:S(2)}) %collective-permute-start.1) | collective-permute-done | bytes 2097184 | tf_op jit(solution)/shard_map/ppermute | solution.py:319
  47.7 4.6 %collective-permute-start.9 = (bf16[128,8192]{1,0:T(8,128)(2,1)}, bf16[128,8192]{1,0:T(8,128)(2,1)S(1)}, u32[]{:S(2)}, u32[]{:S(2)}) collective-permute-start(bf16[128,8192]{1,0:T(8,128)(2,1)} %collective-permute-done.1.refs_13_), channel_id=1, source_target_pairs={{2,4},{6,8},{10,12},{14,16},{18,20},{22,24},{26,28},{5,3},{9,7},{1... | collective-permute-start | bytes 6291464 | tf_op jit(solution)/shard_map/ppermute | solution.py:330
  52.3 1.0 dynamic-slice_select_fusion
  53.4 1.9 %collective-permute-start.3 = (bf16[128,4096]{1,0:T(8,128)(2,1)}, bf16[128,4096]{1,0:T(8,128)(2,1)S(1)}, u32[]{:S(2)}, u32[]{:S(2)}) collective-permute-start(bf16[128,4096]{1,0:T(8,128)(2,1)} %get-tuple-element.16), channel_id=1, source_target_pairs={{1,2},{2,1},{5,6},{6,5},{9,10},{10,9},{13,14},{14,13},{17,18},{18,... | collective-permute-start | bytes 3145736 | tf_op jit(solution)/shard_map/ppermute | solution.py:319
  55.4 0.5 collective-permute-start.6
  55.9 9.5 %collective-permute-done.2.refs_0_ = bf16[128,4096]{1,0:T(8,128)(2,1)S(1)} collective-permute-done((bf16[128,4096]{1,0:T(8,128)(2,1)}, bf16[128,4096]{1,0:T(8,128)(2,1)S(1)}, u32[]{:S(2)}, u32[]{:S(2)}) %collective-permute-start.2) | collective-permute-done | bytes 1048608 | tf_op jit(solution)/shard_map/ppermute | solution.py:319
  65.4 1.3 collective-permute-start.8
  66.7 8.8 %collective-permute-done.9.refs_18_ = bf16[128,8192]{1,0:T(8,128)(2,1)S(1)} collective-permute-done((bf16[128,8192]{1,0:T(8,128)(2,1)}, bf16[128,8192]{1,0:T(8,128)(2,1)S(1)}, u32[]{:S(2)}, u32[]{:S(2)}) %collective-permute-start.9) | collective-permute-done | bytes 2097184 | tf_op jit(solution)/shard_map/ppermute | solution.py:330
  75.5 1.3 collective-permute-start.10
  76.9 1.7 collective-permute-start.13
  78.6 3.1 %collective-permute-start.14 = (bf16[128,4096]{1,0:T(8,128)(2,1)}, bf16[128,4096]{1,0:T(8,128)(2,1)}, u32[]{:S(2)}, u32[]{:S(2)}) collective-permute-start(bf16[128,4096]{1,0:T(8,128)(2,1)} %get-tuple-element.21), channel_id=1, source_target_pairs={{1,2},{2,1},{5,6},{6,5},{9,10},{10,9},{13,14},{14,13},{17,18},{18,... | collective-permute-start | bytes 3145736 | tf_op jit(solution)/shard_map/ppermute | solution.py:319
  81.9 0.1 broadcast_in_dim.14.refs_10_
  82.0 1.1 copy-done.11
  83.1 0.7 copy-done.12
  83.8 0.9 copy-done.4
  84.7 0.9 copy-done.6
  85.6 0.9 copy-done.8
  86.5 33.1 %shard_map.145 = (bf16[128,4096]{1,0:T(8,128)(2,1)}, bf16[128,4096]{1,0:T(8,128)(2,1)S(1)}, f32[49168,128]{1,0:T(8,128)}) custom-call(s32[5]{0:T(128)S(1)} %stack.23.places, s32[40960]{0:T(1024)S(1)} %pad_add_fusion.aux, bf16[128,4096]{1,0:T(8,128)(2,1)S(1)} %collective-permute-done.2.refs_0_, bf16[128,16384]{1,0:T(8,128)(2,1)} %refs_1_.3, ...), custom_call_target="tpu_custom_call" | custom-call | flops 2867200000 | bytes 8388608 | tf_op jit(solution)/shard_map/pallas_call | solution.py:237
  119.6 1.0 copy-done.2
  120.6 2.5 %collective-permute-start.12 = (bf16[128,4096]{1,0:T(8,128)(2,1)}, bf16[128,4096]{1,0:T(8,128)(2,1)S(1)}, u32[]{:S(2)}, u32[]{:S(2)}) collective-permute-start(bf16[128,4096]{1,0:T(8,128)(2,1)} %copy-done.2), channel_id=1, source_target_pairs={{1,2},{2,1},{5,6},{6,5},{9,10},{10,9},{13,14},{14,13},{17,18},{18,... | collective-permute-start | bytes 3145736 | tf_op jit(solution)/shard_map/ppermute | solution.py:319
  123.1 2.2 %copy-done = bf16[128,16384]{1,0:T(8,128)(2,1)S(1)} copy-done((bf16[128,16384]{1,0:T(8,128)(2,1)S(1)}, bf16[128,16384]{1,0:T(8,128)(2,1)}, u32[]{:S(2)}) %copy-start) | copy-done | bytes 4194328
  125.3 0.9 copy-done.5
  126.2 0.9 copy-done.7
  127.1 31.2 %shard_map.146 = (bf16[128,4096]{1,0:T(8,128)(2,1)S(1)}, bf16[128,4096]{1,0:T(8,128)(2,1)S(1)}) custom-call(s32[5]{0:T(128)S(1)} %stack.23.places, s32[40960]{0:T(1024)S(1)} %pad_add_fusion.aux, bf16[128,4096]{1,0:T(8,128)(2,1)} %collective-permute-done.13.refs_0_, bf16[128,16384]{1,0:T(8,128)(2,1)S(1)} %copy-done, ...), custom_call_target="tpu_custom_call" | custom-call | flops 2867200000 | bytes 8388608 | tf_op jit(solution)/shard_map/pallas_call | solution.py:237
  158.4 3.2 %collective-permute-start.16 = (bf16[128,4096]{1,0:T(8,128)(2,1)S(1)}, bf16[128,4096]{1,0:T(8,128)(2,1)S(1)}, u32[]{:S(2)}, u32[]{:S(2)}) collective-permute-start(bf16[128,4096]{1,0:T(8,128)(2,1)S(1)} %get-tuple-element.23), channel_id=1, source_target_pairs={{1,2},{2,1},{5,6},{6,5},{9,10},{10,9},{13,14},{14,13},{17,18},{18,... | collective-permute-start | bytes 3145736 | tf_op jit(solution)/shard_map/ppermute | solution.py:319
  161.6 0.4 broadcast_in_dim.10
  162.0 1.5 select_dynamic-update-slice_fusion.3
  163.6 0.3 select_dynamic-update-slice_fusion.2
  163.9 16.7 %collective-permute-done.15 = bf16[128,4096]{1,0:T(8,128)(2,1)S(1)} collective-permute-done((bf16[128,4096]{1,0:T(8,128)(2,1)S(1)}, bf16[128,4096]{1,0:T(8,128)(2,1)S(1)}, u32[]{:S(2)}, u32[]{:S(2)}) %collective-permute-start.15) | collective-permute-done | bytes 1048608 | tf_op jit(solution)/shard_map/ppermute | solution.py:319
  180.6 0.3 select_dynamic-update-slice_fusion.1
  180.9 2.4 %collective-permute-done.16 = bf16[128,4096]{1,0:T(8,128)(2,1)S(1)} collective-permute-done((bf16[128,4096]{1,0:T(8,128)(2,1)S(1)}, bf16[128,4096]{1,0:T(8,128)(2,1)S(1)}, u32[]{:S(2)}, u32[]{:S(2)}) %collective-permute-start.16) | collective-permute-done | bytes 1048608 | tf_op jit(solution)/shard_map/ppermute | solution.py:319
  183.2 1.2 select_dynamic-update-slice_fusion
  (49 shorter events, 0.7 us)
Async XLA Ops:
  0.0 47.7 %collective-permute-start.1 = (bf16[128,8192]{1,0:T(8,128)(2,1)}, bf16[128,8192]{1,0:T(8,128)(2,1)}, u32[]{:S(2)}, u32[]{:S(2)}) collective-permute-start(bf16[128,8192]{1,0:T(8,128)(2,1)} %refs_12_.1), channel_id=1, source_target_pairs={{0,1},{1,0},{2,3},{3,2},{4,5},{5,4},{6,7},{7,6},{8,9},{9,8},{10,11... | collective-permute-start | bytes 6291464 | tf_op jit(solution)/shard_map/ppermute | solution.py:319
  2.1 53.4 %collective-permute-start.7 = (bf16[128,8192]{1,0:T(8,128)(2,1)}, bf16[128,8192]{1,0:T(8,128)(2,1)}, u32[]{:S(2)}, u32[]{:S(2)}) collective-permute-start(bf16[128,8192]{1,0:T(8,128)(2,1)} %refs_12_.1), channel_id=1, source_target_pairs={{2,4},{6,8},{10,12},{14,16},{18,20},{22,24},{26,28},{5,3},{9,7},{1... | collective-permute-start | bytes 6291464 | tf_op jit(solution)/shard_map/ppermute | solution.py:330
  9.2 44.2 %collective-permute-start = (s32[5,8192]{1,0:T(8,128)S(1)}, s32[5,8192]{1,0:T(8,128)S(1)}, u32[]{:S(2)}, u32[]{:S(2)}) collective-permute-start(s32[5,8192]{1,0:T(8,128)S(1)} %pad_dynamic-slice_fusion), channel_id=1, source_target_pairs={{0,2},{3,1},{4,6},{7,5},{8,10},{11,9},{12,14},{15,13},{16,18},{19,... | collective-permute-start | bytes 491528 | tf_op jit(solution)/shard_map/ppermute | solution.py:319
  12.0 40.3 %collective-permute-start.4 = (f32[4,8192]{1,0:T(4,128)}, f32[4,8192]{1,0:T(4,128)}, u32[]{:S(2)}, u32[]{:S(2)}) collective-permute-start(f32[4,8192]{1,0:T(4,128)} %constant_dynamic-slice_fusion.6), channel_id=1, source_target_pairs={{0,2},{3,1},{4,6},{7,5},{8,10},{11,9},{12,14},{15,13},{16,18},{19,... | collective-permute-start | bytes 393224 | tf_op jit(solution)/shard_map/ppermute | solution.py:319
  19.3 33.0 %copy-start.13 = (f32[4,16384]{1,0:T(4,128)S(1)}, f32[4,16384]{1,0:T(4,128)}, u32[]{:S(2)}) copy-start(f32[4,16384]{1,0:T(4,128)} %param.18) | copy-start | bytes 786436
  19.3 36.0 %copy-start.1 = (bf16[128,8192]{1,0:T(8,128)(2,1)S(1)}, bf16[128,8192]{1,0:T(8,128)(2,1)}, u32[]{:S(2)}) copy-start(bf16[128,8192]{1,0:T(8,128)(2,1)} %refs_12_.1) | copy-start | bytes 6291460
  47.7 27.7 %collective-permute-start.9 = (bf16[128,8192]{1,0:T(8,128)(2,1)}, bf16[128,8192]{1,0:T(8,128)(2,1)S(1)}, u32[]{:S(2)}, u32[]{:S(2)}) collective-permute-start(bf16[128,8192]{1,0:T(8,128)(2,1)} %collective-permute-done.1.refs_13_), channel_id=1, source_target_pairs={{2,4},{6,8},{10,12},{14,16},{18,20},{22,24},{26,28},{5,3},{9,7},{1... | collective-permute-start | bytes 6291464 | tf_op jit(solution)/shard_map/ppermute | solution.py:330
  53.3 12.1 %collective-permute-start.2 = (bf16[128,4096]{1,0:T(8,128)(2,1)}, bf16[128,4096]{1,0:T(8,128)(2,1)S(1)}, u32[]{:S(2)}, u32[]{:S(2)}) collective-permute-start(bf16[128,4096]{1,0:T(8,128)(2,1)} %get-tuple-element.15), channel_id=1, source_target_pairs={{0,2},{3,1},{1,0},{2,3},{4,6},{7,5},{5,4},{6,7},{8,10},{11,9},{9,8... | collective-permute-start | bytes 3145736 | tf_op jit(solution)/shard_map/ppermute | solution.py:319
  53.4 23.5 %collective-permute-start.3 = (bf16[128,4096]{1,0:T(8,128)(2,1)}, bf16[128,4096]{1,0:T(8,128)(2,1)S(1)}, u32[]{:S(2)}, u32[]{:S(2)}) collective-permute-start(bf16[128,4096]{1,0:T(8,128)(2,1)} %get-tuple-element.16), channel_id=1, source_target_pairs={{1,2},{2,1},{5,6},{6,5},{9,10},{10,9},{13,14},{14,13},{17,18},{18,... | collective-permute-start | bytes 3145736 | tf_op jit(solution)/shard_map/ppermute | solution.py:319
  55.3 23.3 %collective-permute-start.5 = (bf16[128,8192]{1,0:T(8,128)(2,1)S(1)}, bf16[128,8192]{1,0:T(8,128)(2,1)S(1)}, u32[]{:S(2)}, u32[]{:S(2)}) collective-permute-start(bf16[128,8192]{1,0:T(8,128)(2,1)S(1)} %copy-done.1), channel_id=1, source_target_pairs={{0,2},{1,3},{2,0},{3,1},{4,6},{5,7},{6,4},{7,5},{8,10},{9,11},{10,... | collective-permute-start | bytes 6291464 | tf_op jit(solution)/shard_map/ppermute | solution.py:319
  55.4 26.3 %collective-permute-start.6 = (bf16[128,8192]{1,0:T(8,128)(2,1)}, bf16[128,8192]{1,0:T(8,128)(2,1)S(1)}, u32[]{:S(2)}, u32[]{:S(2)}) collective-permute-start(bf16[128,8192]{1,0:T(8,128)(2,1)} %collective-permute-done.1.refs_13_), channel_id=1, source_target_pairs={{0,2},{1,3},{2,0},{3,1},{4,6},{5,7},{6,4},{7,5},{8,10},{9,11},{10,... | collective-permute-start | bytes 6291464 | tf_op jit(solution)/shard_map/ppermute | solution.py:319
  65.4 16.4 %collective-permute-start.8 = (bf16[128,8192]{1,0:T(8,128)(2,1)}, bf16[128,8192]{1,0:T(8,128)(2,1)S(1)}, u32[]{:S(2)}, u32[]{:S(2)}) collective-permute-start(bf16[128,8192]{1,0:T(8,128)(2,1)} %collective-permute-done.7.refs_16_), channel_id=1, source_target_pairs={{0,2},{3,1},{4,6},{7,5},{8,10},{11,9},{12,14},{15,13},{16,18},{19,... | collective-permute-start | bytes 6291464 | tf_op jit(solution)/shard_map/ppermute | solution.py:319
  75.5 6.6 %copy-start.10 = (bf16[128,8192]{1,0:T(8,128)(2,1)}, bf16[128,8192]{1,0:T(8,128)(2,1)S(1)}, u32[]{:S(2)}) copy-start(bf16[128,8192]{1,0:T(8,128)(2,1)S(1)} %collective-permute-done.9.refs_18_) | copy-start | bytes 6291460
  75.5 6.3 %collective-permute-start.10 = (bf16[128,8192]{1,0:T(8,128)(2,1)S(1)}, bf16[128,8192]{1,0:T(8,128)(2,1)S(1)}, u32[]{:S(2)}, u32[]{:S(2)}) collective-permute-start(bf16[128,8192]{1,0:T(8,128)(2,1)S(1)} %collective-permute-done.9.refs_18_), channel_id=1, source_target_pairs={{0,2},{3,1},{4,6},{7,5},{8,10},{11,9},{12,14},{15,13},{16,18},{19,... | collective-permute-start | bytes 6291464 | tf_op jit(solution)/shard_map/ppermute | solution.py:319
  76.9 46.1 %collective-permute-start.13 = (bf16[128,4096]{1,0:T(8,128)(2,1)}, bf16[128,4096]{1,0:T(8,128)(2,1)}, u32[]{:S(2)}, u32[]{:S(2)}) collective-permute-start(bf16[128,4096]{1,0:T(8,128)(2,1)} %get-tuple-element.20), channel_id=1, source_target_pairs={{0,2},{3,1},{1,0},{2,3},{4,6},{7,5},{5,4},{6,7},{8,10},{11,9},{9,8... | collective-permute-start | bytes 3145736 | tf_op jit(solution)/shard_map/ppermute | solution.py:319
  78.6 44.4 %collective-permute-start.14 = (bf16[128,4096]{1,0:T(8,128)(2,1)}, bf16[128,4096]{1,0:T(8,128)(2,1)}, u32[]{:S(2)}, u32[]{:S(2)}) collective-permute-start(bf16[128,4096]{1,0:T(8,128)(2,1)} %get-tuple-element.21), channel_id=1, source_target_pairs={{1,2},{2,1},{5,6},{6,5},{9,10},{10,9},{13,14},{14,13},{17,18},{18,... | collective-permute-start | bytes 3145736 | tf_op jit(solution)/shard_map/ppermute | solution.py:319
  81.8 1.3 copy-start.11
  81.8 2.0 %copy-start.12 = (bf16[128,8192]{1,0:T(8,128)(2,1)}, bf16[128,8192]{1,0:T(8,128)(2,1)S(1)}, u32[]{:S(2)}) copy-start(bf16[128,8192]{1,0:T(8,128)(2,1)S(1)} %collective-permute-done.10.refs_19_) | copy-start | bytes 6291460
  83.8 0.9 copy-start.4
  84.7 0.9 copy-start.6
  85.6 0.9 copy-start.8
  119.6 1.0 copy-start.2
  120.6 41.0 %collective-permute-start.11 = (bf16[128,4096]{1,0:T(8,128)(2,1)}, bf16[128,4096]{1,0:T(8,128)(2,1)}, u32[]{:S(2)}, u32[]{:S(2)}) collective-permute-start(bf16[128,4096]{1,0:T(8,128)(2,1)} %get-tuple-element.19), channel_id=1, source_target_pairs={{2,0},{1,3},{0,1},{3,2},{6,4},{5,7},{4,5},{7,6},{10,8},{9,11},{8,9... | collective-permute-start | bytes 3145736 | tf_op jit(solution)/shard_map/ppermute | solution.py:319
  120.6 43.0 %collective-permute-start.12 = (bf16[128,4096]{1,0:T(8,128)(2,1)}, bf16[128,4096]{1,0:T(8,128)(2,1)S(1)}, u32[]{:S(2)}, u32[]{:S(2)}) collective-permute-start(bf16[128,4096]{1,0:T(8,128)(2,1)} %copy-done.2), channel_id=1, source_target_pairs={{1,2},{2,1},{5,6},{6,5},{9,10},{10,9},{13,14},{14,13},{17,18},{18,... | collective-permute-start | bytes 3145736 | tf_op jit(solution)/shard_map/ppermute | solution.py:319
  123.1 2.2 %copy-start = (bf16[128,16384]{1,0:T(8,128)(2,1)S(1)}, bf16[128,16384]{1,0:T(8,128)(2,1)}, u32[]{:S(2)}) copy-start(bf16[128,16384]{1,0:T(8,128)(2,1)} %refs_1_.3) | copy-start | bytes 12582916
  125.3 0.9 copy-start.5
  126.2 0.9 copy-start.7
  158.3 3.7 %copy-start.3 = (bf16[128,4096]{1,0:T(8,128)(2,1)S(1)}, bf16[128,4096]{1,0:T(8,128)(2,1)}, u32[]{:S(2)}) copy-start(bf16[128,4096]{1,0:T(8,128)(2,1)} %copy-done.2) | copy-start | bytes 3145732
  158.3 22.2 %collective-permute-start.15 = (bf16[128,4096]{1,0:T(8,128)(2,1)S(1)}, bf16[128,4096]{1,0:T(8,128)(2,1)S(1)}, u32[]{:S(2)}, u32[]{:S(2)}) collective-permute-start(bf16[128,4096]{1,0:T(8,128)(2,1)S(1)} %get-tuple-element.24), channel_id=1, source_target_pairs={{2,0},{1,3},{0,1},{3,2},{6,4},{5,7},{4,5},{7,6},{10,8},{9,11},{8,9... | collective-permute-start | bytes 3145736 | tf_op jit(solution)/shard_map/ppermute | solution.py:319
  158.4 24.9 %collective-permute-start.16 = (bf16[128,4096]{1,0:T(8,128)(2,1)S(1)}, bf16[128,4096]{1,0:T(8,128)(2,1)S(1)}, u32[]{:S(2)}, u32[]{:S(2)}) collective-permute-start(bf16[128,4096]{1,0:T(8,128)(2,1)S(1)} %get-tuple-element.23), channel_id=1, source_target_pairs={{1,2},{2,1},{5,6},{6,5},{9,10},{10,9},{13,14},{14,13},{17,18},{18,... | collective-permute-start | bytes 3145736 | tf_op jit(solution)/shard_map/ppermute | solution.py:319
  180.9 2.4 %copy-start.9 = (bf16[128,16384]{1,0:T(8,128)(2,1)}, bf16[128,16384]{1,0:T(8,128)(2,1)S(1)}, u32[]{:S(2)}) copy-start(bf16[128,16384]{1,0:T(8,128)(2,1)S(1)} %select_dynamic-update-slice_fusion.1) | copy-start | bytes 12582916
